TPU v7x, 256 devices: a whole 4x4x8 slice. The times are simulated.
256 devices in a mesh: pts: 32 (over x, z), dp: 8 (over y, core).
Axes of the slice: x: 4, y: 4, z: 8, core: 2. Of those that a mesh axis runs over, the one named last changes fastest.
Arguments:
- features: bfloat16 [131072, 256], P(('dp', 'pts')), parts along dimension 0, may hold values from -640 to 640
- morton_order: int32 [131072], P(('dp', 'pts')), parts along dimension 0, may hold values from 0 to 16383, as said below
- hilbert_order: int32 [131072], P(('dp', 'pts')), parts along dimension 0, may hold values from 0 to 16383, as said below
- cotangent: bfloat16 [131072, 256], P(('dp', 'pts')), parts along dimension 0, may hold values from -6 to 6
- norm_gains: bfloat16 [2, 2, 256], replicated, may hold values from 0.099609375 to 1.8984375
- qkv_weight: bfloat16 [2, 256, 768], replicated, may hold values from -0.375 to 0.375
- proj_weight: bfloat16 [2, 256, 256], replicated, may hold values from -0.375 to 0.375
- expand_weight: bfloat16 [2, 256, 1024], replicated, may hold values from -0.375 to 0.375
- contract_weight: bfloat16 [2, 1024, 256], replicated, may hold values from -0.1875 to 0.1875
Outputs:
- block_output: bfloat16 [131072, 256], P(('dp', 'pts')), parts along dimension 0
- feature_grad: bfloat16 [131072, 256], P(('dp', 'pts')), parts along dimension 0
- gain_grad: float32 [16, 256], P('dp', 'pts'), parts along dimension 0
- qkv_grad: float32 [2048, 768], P(('dp', 'pts')), parts along dimension 0
- proj_grad: float32 [2048, 256], P(('dp', 'pts')), parts along dimension 0
- expand_grad: float32 [2048, 1024], P(('dp', 'pts')), parts along dimension 0
- contract_grad: float32 [8192, 256], P(('dp', 'pts')), parts along dimension 0
There are 8 independent parts, one for each index of `dp`. A program takes and returns all parts, laid end to end along the dimension named above; an argument that names none is the same for every part. Nothing has to cross between parts.
Inputs may be any that keep to these rules, and one draw needn't show every extreme that they name: A permutation of the stored rows: Z-order position j holds stored row morton_order[j]. With positions and stored rows taken in aligned blocks of 512, each block of positions takes 1 to 31 rows from each block of stored rows, exactly 31 for some pairs in every draw, and the counts from each block of stored rows to the blocks of positions are a rearrangement of one list. A permutation of the Z-order positions: Hilbert position j holds Z-order position hilbert_order[j]. The same bounds hold between aligned blocks of 512 Hilbert positions and of 512 Z-order positions.
All inputs are finite; a program needn't handle non-finite values.
Results may differ from a plain program's by a relative error of at most 0.034.
Values may be sent and summed in bfloat16 or wider, within the bound.
A program may use at most 128 MiB of HBM per device.

v0:
```python
import jax
import jax.numpy as jnp
from jax import lax
from jax.sharding import PartitionSpec as P

D = 256
HEADS = 8
PATCH = 512
HD = 32


def layer_norm(values, gain):
    center = values - jnp.mean(values, axis=-1, keepdims=True)
    spread = jnp.mean(center * center, axis=-1, keepdims=True)
    return center * lax.rsqrt(spread + 1e-05) * gain.astype(jnp.float32)


def head_attention(head_packed):
    scores = jnp.dot(
        head_packed[:, 0], head_packed[:, 1].T, preferred_element_type=jnp.float32
    ) * HD ** (-0.5)
    expon = jnp.exp(scores)
    attn = (expon / jnp.sum(expon, axis=-1, keepdims=True)).astype(jnp.bfloat16)
    return jnp.dot(attn, head_packed[:, 2], preferred_element_type=jnp.float32).astype(jnp.bfloat16)


def patch_attention(packed):
    heads_first = jnp.moveaxis(packed, 2, 0)
    mixed = lax.map(head_attention, heads_first)
    return jnp.moveaxis(mixed, 0, 1).reshape(PATCH, D)


def block_apply(point_rows, params):
    gains, qkv_w, proj_w, expand_w, contract_w = params
    resid = point_rows.astype(jnp.float32)
    normed = layer_norm(resid, gains[0]).astype(jnp.bfloat16)
    packed = jnp.dot(normed, qkv_w, preferred_element_type=jnp.float32).astype(jnp.bfloat16)
    packed = packed.reshape(-1, PATCH, 3, HEADS, HD)
    mixed = lax.map(patch_attention, packed).reshape(-1, D)
    after_attn = resid + jnp.dot(mixed, proj_w, preferred_element_type=jnp.float32)
    normed_two = layer_norm(after_attn, gains[1]).astype(jnp.bfloat16)
    hidden = jax.nn.gelu(
        jnp.dot(normed_two, expand_w, preferred_element_type=jnp.float32), approximate=False
    ).astype(jnp.bfloat16)
    return (after_attn + jnp.dot(hidden, contract_w, preferred_element_type=jnp.float32)).astype(
        jnp.bfloat16
    )


def plan_requests(ordering, row_count, peer_count, slot_cap):
    source = ordering // row_count
    local_index = ordering % row_count
    peer_ids = jnp.arange(peer_count, dtype=jnp.int32)
    member = (source[:, None] == peer_ids[None, :]).astype(jnp.int32)
    earlier = jnp.cumsum(member, axis=0) - member
    slot_index = jnp.sum(earlier * member, axis=1)
    placement = source * slot_cap + slot_index
    wanted = jnp.full((peer_count * slot_cap,), row_count, jnp.int32).at[placement].set(local_index)
    return (wanted.reshape(peer_count, slot_cap), placement)


def send_requests(asked):
    return lax.all_to_all(asked, "pts", split_axis=0, concat_axis=0, tiled=True)


def fetch_rows(values, wanted, placement):
    peer_count, slot_cap = wanted.shape
    channels = values.shape[1]
    outgoing = jnp.take(values, wanted.reshape(-1), axis=0, mode="fill", fill_value=0).reshape(
        peer_count, slot_cap, channels
    )
    incoming = lax.all_to_all(outgoing, "pts", split_axis=0, concat_axis=0, tiled=True)
    return jnp.take(incoming.reshape(peer_count * slot_cap, channels), placement, axis=0)


def return_rows(row_grads, wanted, placement, row_count):
    peer_count, slot_cap = wanted.shape
    channels = row_grads.shape[1]
    outgoing = (
        jnp.zeros((peer_count * slot_cap, channels), row_grads.dtype).at[placement].set(row_grads)
    )
    incoming = lax.all_to_all(
        outgoing.reshape(peer_count, slot_cap, channels),
        "pts",
        split_axis=0,
        concat_axis=0,
        tiled=True,
    )
    landed = jnp.zeros((row_count, channels), row_grads.dtype)
    return landed.at[wanted.reshape(-1)].set(
        incoming.reshape(peer_count * slot_cap, channels), mode="drop"
    )


def per_device(
    features,
    morton_order,
    hilbert_order,
    cotangent,
    norm_gains,
    qkv_weight,
    proj_weight,
    expand_weight,
    contract_weight,
):
    row_count = features.shape[0]
    peer_count = lax.axis_size("pts")
    slot_cap = 2 * row_count // peer_count - 1
    morton_ask, morton_place = plan_requests(morton_order, row_count, peer_count, slot_cap)
    hilbert_ask, hilbert_place = plan_requests(hilbert_order, row_count, peer_count, slot_cap)
    morton_wanted = send_requests(morton_ask)
    hilbert_wanted = send_requests(hilbert_ask)
    stacked = (norm_gains, qkv_weight, proj_weight, expand_weight, contract_weight)
    first_params = tuple((weight_set[0] for weight_set in stacked))
    second_params = tuple((weight_set[1] for weight_set in stacked))

    def first_block(rows_in):
        return block_apply(rows_in, first_params)

    morton_rows = fetch_rows(features, morton_wanted, morton_place)
    morton_out, first_pullback = jax.vjp(first_block, morton_rows)
    hilbert_rows = fetch_rows(morton_out, hilbert_wanted, hilbert_place)
    block_output, second_pullback = jax.vjp(block_apply, hilbert_rows, second_params)
    hilbert_grad, second_grads = second_pullback(cotangent)
    terms = tuple((grad_part.astype(jnp.float32) for grad_part in second_grads))
    morton_grad = return_rows(hilbert_grad, hilbert_wanted, hilbert_place, row_count)
    morton_row_grad = first_pullback(morton_grad)[0]
    feature_grad = return_rows(morton_row_grad, morton_wanted, morton_place, row_count)
    grad_out = (
        lax.psum_scatter(
            terms[0].astype(jnp.bfloat16), "pts", scatter_dimension=1, tiled=True
        ).astype(jnp.float32),
        lax.psum_scatter(
            terms[1].astype(jnp.bfloat16), "pts", scatter_dimension=0, tiled=True
        ).astype(jnp.float32),
        lax.psum_scatter(
            terms[2].astype(jnp.bfloat16), "pts", scatter_dimension=0, tiled=True
        ).astype(jnp.float32),
        lax.psum_scatter(
            terms[3].astype(jnp.bfloat16), "pts", scatter_dimension=0, tiled=True
        ).astype(jnp.float32),
        lax.psum_scatter(
            terms[4].astype(jnp.bfloat16), "pts", scatter_dimension=0, tiled=True
        ).astype(jnp.float32),
    )
    return (block_output, feature_grad) + tuple(grad_out)


def solution(mesh):
    placed = (
        P(("dp", "pts"), None),
        P(("dp", "pts")),
        P(("dp", "pts")),
        P(("dp", "pts"), None),
        P(),
        P(),
        P(),
        P(),
        P(),
    )
    return jax.shard_map(
        per_device,
        mesh=mesh,
        in_specs=placed,
        out_specs=(
            P(("dp", "pts"), None),
            P(("dp", "pts"), None),
            P("dp", "pts"),
            P(("dp", "pts"), None),
            P(("dp", "pts"), None),
            P(("dp", "pts"), None),
            P(("dp", "pts"), None),
        ),
        check_vma=False,
    )
```

profile of v0, /device:TPU:22, one launch (start us, length us, event | category | flops | bytes accessed | tf_op | source)
XLA Modules:
  0.0 1032.6 jit_solution(16411944525839126736)
XLA Ops:
  9.5 2.4 scatter_custom_fusion
  12.7 11.6 %all-to-all-start = ((s32[32,1,31]{2,1,0:T(1,128)}), s32[32,1,31]{2,1,0:T(1,128)S(1)}, u32[]{:S(2)}, u32[]{:S(2)}) async-start(s32[32,1,31]{2,1,0:T(1,128)} %bitcast.53), calls=%async_computation | async-start | bytes 32768 | tf_op jit(solution)/shard_map/all_to_all | solution.py:63
  26.5 2.4 scatter_custom_fusion.1
  29.7 2.4 all-to-all-done
  32.1 7.4 all-to-all-start.2
  40.9 4.1 gather_fusion
  47.3 8.9 all-to-all-start.1
  57.1 13.0 %all-to-all-done.1 = bf16[32,31,256]{2,1,0:T(8,128)(2,1)S(1)} async-done(((bf16[32,31,256]{2,1,0:T(8,128)(2,1)}), bf16[32,31,256]{2,1,0:T(8,128)(2,1)S(1)}, u32[]{:S(2)}, u32[]{:S(2)}) %all-to-all-start.1) | async-done | bytes 507936 | tf_op jit(solution)/shard_map/all_to_all | solution.py:72
  70.3 2.0 gather_fusion.1
  74.4 4.3 broadcast.449.clone
  78.7 2.3 broadcast.451.clone
  81.2 21.3 %while.132 = (s32[]{:T(128)}, bf16[8,512,32]{1,2,0:T(8,128)(2,1)S(1)}, bf16[8,32,512]{2,1,0:T(8,128)(2,1)S(1)}, bf16[8,512,32]{1,2,0:T(8,128)(2,1)S(1)}, f32[8,5...) while((s32[]{:T(128)}, ...), condition=%wide.region_8.11_spmd, body=%wide.region_6.10_spmd.sunk | while | flops 35144192 | bytes 6304897 | solution.py:29
  103.7 5.7 fusion.85
  112.1 4.1 gather_fusion.2
  117.3 7.3 all-to-all-start.3
  125.0 13.1 %all-to-all-done.3 = bf16[32,31,256]{2,1,0:T(8,128)(2,1)S(1)} async-done(((bf16[32,31,256]{2,1,0:T(8,128)(2,1)}), bf16[32,31,256]{2,1,0:T(8,128)(2,1)S(1)}, u32[]{:S(2)}, u32[]{:S(2)}) %all-to-all-start.3) | async-done | bytes 507936 | tf_op jit(solution)/shard_map/all_to_all | solution.py:72
  138.3 2.0 gather_fusion.3
  140.6 2.4 convolution_convert_fusion.12
  143.0 2.3 copy.70
  145.4 4.3 broadcast.449
  149.6 2.3 broadcast.451
  152.1 28.3 %while.133 = (s32[]{:T(128)}, bf16[8,512,32]{1,2,0:T(8,128)(2,1)S(1)}, bf16[8,32,512]{2,1,0:T(8,128)(2,1)S(1)}, bf16[8,512,32]{1,2,0:T(8,128)(2,1)S(1)}, f32[8,5...) while((s32[]{:T(128)}, ...), condition=%wide.region_19.22_spmd, body=%wide.region_17.21_spmd.sunk | while | flops 35144192 | bytes 6304897 | solution.py:29
  181.6 6.9 multiply_convert_fusion
  193.9 53.6 %while.134 = (s32[]{:T(128)}, bf16[8,512,3,32]{1,3,0,2:T(8,128)(2,1)}, bf16[8,512,512]{1,2,0:T(8,128)(2,1)}, bf16[8,512,32]{2,1,0:T(8,128)(2,1)S(1)}, bf16[8,512...) while((s32[]{:T(128)}, ...), condition=%wide.region_26.29_spmd, body=%wide.region_24.28_spmd.sunk | while | flops 71385088 | bytes 5927561 | solution.py:29
  193.9 1.6 fusion.277
  200.5 1.6 fusion.277
  202.2 1.6 fusion.279
  207.2 1.6 fusion.277
  214.0 1.6 fusion.277
  220.7 1.6 fusion.277
  223.8 1.6 fusion.278
  227.4 1.6 fusion.277
  234.1 1.6 fusion.277
  235.7 1.6 fusion.279
  240.8 1.6 fusion.277
  242.4 1.6 fusion.279
  247.5 1.7 fusion.135
  249.2 2.3 convolution_convert_fusion.16
  252.3 2.5 convolution_convert_fusion.15
  257.0 2.6 scatter_custom_fusion.2
  260.5 7.3 all-to-all-start.4
  269.4 11.8 %all-to-all-done.4 = bf16[32,31,256]{2,1,0:T(8,128)(2,1)S(1)} async-done(((bf16[32,31,256]{2,1,0:T(8,128)(2,1)}), bf16[32,31,256]{2,1,0:T(8,128)(2,1)S(1)}, u32[]{:S(2)}, u32[]{:S(2)}) %all-to-all-start.4) | async-done | bytes 507936 | tf_op jit(solution)/shard_map/all_to_all | solution.py:82
  281.4 5.6 scatter_custom_fusion.3
  287.0 3.7 multiply_reduce_fusion.1
  293.4 53.6 %while.135 = (s32[]{:T(128)}, bf16[8,512,3,32]{1,3,0,2:T(8,128)(2,1)}, bf16[8,512,512]{1,2,0:T(8,128)(2,1)}, bf16[8,512,32]{2,1,0:T(8,128)(2,1)S(1)}, bf16[8,512...) while((s32[]{:T(128)}, ...), condition=%wide.region_35.38_spmd, body=%wide.region_33.37_spmd.sunk | while | flops 71385088 | bytes 5927561 | solution.py:29
  293.4 1.6 fusion.287
  300.1 1.6 fusion.287
  306.8 1.6 fusion.287
  313.5 1.6 fusion.287
  320.2 1.6 fusion.287
  326.9 1.6 fusion.287
  328.5 1.6 fusion.289
  333.6 1.6 fusion.287
  335.3 1.6 fusion.289
  340.3 1.6 fusion.287
  347.0 1.7 fusion.133
  349.3 2.7 scatter_custom_fusion.4
  353.0 6.8 all-to-all-start.5
  361.3 1.6 fusion.100
  363.7 63.0 %all-reduce.8 = bf16[2,256]{1,0:T(2,128)(2,1)S(1)} all-reduce(bf16[2,256]{1,0:T(2,128)(2,1)S(1)} %pad_add_fusion), channel_id=2, replica_groups=mesh['pts'=32,'dp'=8] {'pts'}, use_global_device_ids=true, to_apply=%region_42.45.clone | all-reduce | flops 512 | bytes 2048
  428.5 158.8 %reduce-scatter.6.cloned.1.call-done = bf16[8,768]{1,0:T(8,128)(2,1)} async-done(((bf16[256,768]{1,0:T(8,128)(2,1)}), bf16[8,768]{1,0:T(8,128)(2,1)}) %reduce-scatter.6.cloned.1.call-update) | async-done | bytes 12304 | tf_op jit(solution)/shard_map/reduce_scatter | solution.py:133
  588.6 214.7 %reduce-scatter.10.cloned.1.call-done = bf16[8,1024]{1,0:T(8,128)(2,1)} async-done(((bf16[256,1024]{1,0:T(8,128)(2,1)}), bf16[8,1024]{1,0:T(8,128)(2,1)}) %reduce-scatter.10.cloned.1.call-update) | async-done | bytes 16400 | tf_op jit(solution)/shard_map/reduce_scatter | solution.py:139
  804.6 213.7 %reduce-scatter.12.cloned.1.call-done = bf16[32,256]{1,0:T(8,128)(2,1)} async-done(((bf16[1024,256]{1,0:T(8,128)(2,1)}), bf16[32,256]{1,0:T(8,128)(2,1)}) %reduce-scatter.12.cloned.1.call-update) | async-done | bytes 16400 | tf_op jit(solution)/shard_map/reduce_scatter | solution.py:142
  1019.8 6.0 scatter_custom_fusion.5
  (427 shorter events, 163.5 us)
Async XLA Ops:
  7.2 33.7 %copy-start = (bf16[512,256]{1,0:T(8,128)(2,1)S(1)}, bf16[512,256]{1,0:T(8,128)(2,1)}, u32[]{:S(2)}) copy-start(bf16[512,256]{1,0:T(8,128)(2,1)} %param.21) | copy-start | bytes 786436
  9.5 46.7 %copy-start.30 = (s32[512]{0:T(512)}, s32[512]{0:T(512)S(1)}, u32[]{:S(2)}) copy-start(s32[512]{0:T(512)S(1)} %get-tuple-element.875) | copy-start | bytes 6148
  12.7 19.4 %all-to-all-start = ((s32[32,1,31]{2,1,0:T(1,128)}), s32[32,1,31]{2,1,0:T(1,128)S(1)}, u32[]{:S(2)}, u32[]{:S(2)}) async-start(s32[32,1,31]{2,1,0:T(1,128)} %bitcast.53), calls=%async_computation | async-start | bytes 32768 | tf_op jit(solution)/shard_map/all_to_all | solution.py:63
  26.5 98.5 %copy-start.31 = (s32[512]{0:T(512)}, s32[512]{0:T(512)S(1)}, u32[]{:S(2)}) copy-start(s32[512]{0:T(512)S(1)} %get-tuple-element.873) | copy-start | bytes 6148
  32.1 15.2 %all-to-all-start.2 = ((s32[32,1,31]{2,1,0:T(1,128)}), s32[32,1,31]{2,1,0:T(1,128)S(1)}, u32[]{:S(2)}, u32[]{:S(2)}) async-start(s32[32,1,31]{2,1,0:T(1,128)} %bitcast.50), calls=%async_computation.2 | async-start | bytes 32768 | tf_op jit(solution)/shard_map/all_to_all | solution.py:63
  44.9 11.3 %copy-start.32 = (bf16[2,2,256]{2,1,0:T(2,128)(2,1)S(1)}, bf16[2,2,256]{2,1,0:T(2,128)(2,1)}, u32[]{:S(2)}) copy-start(bf16[2,2,256]{2,1,0:T(2,128)(2,1)} %param.25) | copy-start | bytes 6148
  47.3 22.8 %all-to-all-start.1 = ((bf16[32,31,256]{2,1,0:T(8,128)(2,1)}), bf16[32,31,256]{2,1,0:T(8,128)(2,1)S(1)}, u32[]{:S(2)}, u32[]{:S(2)}) async-start(bf16[32,31,256]{2,1,0:T(8,128)(2,1)} %reshape.428), calls=%async_computation.1 | async-start | bytes 1048576 | tf_op jit(solution)/shard_map/all_to_all | solution.py:72
  56.2 16.4 %copy-start.33 = (f32[1,1,256]{2,1,0:T(1,128)}, f32[1,1,256]{2,1,0:T(1,128)S(1)}, u32[]{:S(2)}) copy-start(f32[1,1,256]{2,1,0:T(1,128)S(1)} %get-tuple-element.898) | copy-start | bytes 3076
  56.2 47.4 %copy-start.35 = (f32[1,1,256]{2,1,0:T(1,128)}, f32[1,1,256]{2,1,0:T(1,128)S(1)}, u32[]{:S(2)}) copy-start(f32[1,1,256]{2,1,0:T(1,128)S(1)} %get-tuple-element.897) | copy-start | bytes 3076
  56.3 84.4 %copy-start.23 = (f32[1,1,256]{2,1,0:T(1,128)}, f32[1,1,256]{2,1,0:T(1,128)S(1)}, u32[]{:S(2)}) copy-start(f32[1,1,256]{2,1,0:T(1,128)S(1)} %get-tuple-element.899) | copy-start | bytes 3076
  56.3 134.6 %copy-start.26 = (f32[1,1,256]{2,1,0:T(1,128)}, f32[1,1,256]{2,1,0:T(1,128)S(1)}, u32[]{:S(2)}) copy-start(f32[1,1,256]{2,1,0:T(1,128)S(1)} %get-tuple-element.896) | copy-start | bytes 3076
  81.2 22.1 %copy-start.6 = (bf16[2,256,256]{2,1,0:T(8,128)(2,1)S(1)}, bf16[2,256,256]{2,1,0:T(8,128)(2,1)}, u32[]{:S(2)}) copy-start(bf16[2,256,256]{2,1,0:T(8,128)(2,1)} %param.27) | copy-start | bytes 786436
  102.5 0.7 copy-start.19
  102.5 0.8 copy-start.20
  102.5 6.9 copy-start.14
  103.7 5.8 copy-start.28
  103.7 7.7 copy-start.11
  109.4 1.4 copy-start.4
  109.4 2.0 copy-start.5
  116.1 8.7 copy-start.15
  117.3 20.8 %all-to-all-start.3 = ((bf16[32,31,256]{2,1,0:T(8,128)(2,1)}), bf16[32,31,256]{2,1,0:T(8,128)(2,1)S(1)}, u32[]{:S(2)}, u32[]{:S(2)}) async-start(bf16[32,31,256]{2,1,0:T(8,128)(2,1)} %reshape.433), calls=%async_computation.3 | async-start | bytes 1048576 | tf_op jit(solution)/shard_map/all_to_all | solution.py:72
  124.6 302.7 %reduce-scatter.8.cloned.1.call-start = ((), (), s32[]{:S(2)}) async-start(), calls=%async_computation.11 | async-start | bytes 135168 | tf_op jit(solution)/shard_map/reduce_scatter | solution.py:136
  125.0 67.0 %copy-start.2 = (bf16[512,256]{0,1:T(8,128)(2,1)}, bf16[512,256]{0,1:T(8,128)(2,1)S(1)}, u32[]{:S(2)}) copy-start(bf16[512,256]{0,1:T(8,128)(2,1)S(1)} %copy.73) | copy-start | bytes 786436
  180.4 0.7 copy-start.13
  180.4 0.8 copy-start.17
  180.4 8.1 copy-start.18
  181.6 9.3 copy-start.21
  181.6 6.9 copy-start.12
  188.5 1.2 copy-start.37
  189.8 1.3 copy-start.10
  192.3 395.0 %reduce-scatter.6.cloned.1.call-start = ((), (), s32[]{:S(2)}) async-start(), calls=%async_computation.10 | async-start | bytes 405504 | tf_op jit(solution)/shard_map/reduce_scatter | solution.py:133
  193.9 53.6 %copy-start.24 = (f32[1,1,256]{2,1,0:T(1,128)S(1)}, f32[1,1,256]{2,1,0:T(1,128)}, u32[]{:S(2)}) copy-start(f32[1,1,256]{2,1,0:T(1,128)} %copy-done.23) | copy-start | bytes 3076
  247.5 4.5 copy-start.25
  249.2 3.1 copy-start.22
  249.2 3.1 copy-start.27
  251.5 3.3 copy-start.3
  251.5 551.8 %reduce-scatter.10.cloned.1.call-start = ((), (), s32[]{:S(2)}) async-start(), calls=%async_computation.12 | async-start | bytes 540672 | tf_op jit(solution)/shard_map/reduce_scatter | solution.py:139
  255.8 12.2 %copy-start.8 = (bf16[512,1024]{1,0:T(8,128)(2,1)S(1)}, bf16[512,1024]{1,0:T(8,128)(2,1)}, u32[]{:S(2)}) copy-start(bf16[512,1024]{1,0:T(8,128)(2,1)} %get-tuple-element.870) | copy-start | bytes 3145732
  255.8 12.2 %copy-start.16 = (bf16[512,256]{1,0:T(8,128)(2,1)S(1)}, bf16[512,256]{1,0:T(8,128)(2,1)}, u32[]{:S(2)}) copy-start(bf16[512,256]{1,0:T(8,128)(2,1)} %param.24) | copy-start | bytes 786436
  260.5 20.7 %all-to-all-start.4 = ((bf16[32,31,256]{2,1,0:T(8,128)(2,1)}), bf16[32,31,256]{2,1,0:T(8,128)(2,1)S(1)}, u32[]{:S(2)}, u32[]{:S(2)}) async-start(bf16[32,31,256]{2,1,0:T(8,128)(2,1)} %reshape.440), calls=%async_computation.4 | async-start | bytes 1048576 | tf_op jit(solution)/shard_map/all_to_all | solution.py:82
  267.8 19.1 %copy-start.36 = (f32[1,1,256]{2,1,0:T(1,128)S(1)}, f32[1,1,256]{2,1,0:T(1,128)}, u32[]{:S(2)}) copy-start(f32[1,1,256]{2,1,0:T(1,128)} %copy-done.35) | copy-start | bytes 3076
  267.8 750.5 %reduce-scatter.12.cloned.1.call-start = ((), (), s32[]{:S(2)}) async-start(), calls=%async_computation.13 | async-start | bytes 540672 | tf_op jit(solution)/shard_map/reduce_scatter | solution.py:142
  287.0 3.9 copy-start.29
  290.7 1.0 copy-start.7
  293.4 53.6 %copy-start.34 = (f32[1,1,256]{2,1,0:T(1,128)S(1)}, f32[1,1,256]{2,1,0:T(1,128)}, u32[]{:S(2)}) copy-start(f32[1,1,256]{2,1,0:T(1,128)} %copy-done.33) | copy-start | bytes 3076
  348.9 10.9 %copy-start.38 = (u32[256]{0:T(256)S(1)}, u32[256]{0:T(256)}, u32[]{:S(2)}) copy-start(u32[256]{0:T(256)} %constant.461) | copy-start | bytes 3076
  348.9 12.3 %copy-start.39 = (bf16[256]{0:T(256)(128)(2,1)S(1)}, bf16[256]{0:T(256)(128)(2,1)}, u32[]{:S(2)}) copy-start(bf16[256]{0:T(256)(128)(2,1)} %get-tuple-element.782) | copy-start | bytes 1540
  349.1 12.1 %copy-start.9 = (bf16[512,1024]{1,0:T(8,128)(2,1)S(1)}, bf16[512,1024]{1,0:T(8,128)(2,1)}, u32[]{:S(2)}) copy-start(bf16[512,1024]{1,0:T(8,128)(2,1)} %get-tuple-element.870) | copy-start | bytes 3145732
  353.0 666.7 %all-to-all-start.5 = ((bf16[32,31,256]{2,1,0:T(8,128)(2,1)}), bf16[32,31,256]{2,1,0:T(8,128)(2,1)S(1)}, u32[]{:S(2)}, u32[]{:S(2)}) async-start(bf16[32,31,256]{2,1,0:T(8,128)(2,1)} %reshape.444), calls=%async_computation.5 | async-start | bytes 1048576 | tf_op jit(solution)/shard_map/all_to_all | solution.py:82
  361.2 664.6 %copy-start.1 = (bf16[512,256]{1,0:T(8,128)(2,1)S(1)}, bf16[512,256]{1,0:T(8,128)(2,1)}, u32[]{:S(2)}) copy-start(bf16[512,256]{1,0:T(8,128)(2,1)} %param.21) | copy-start | bytes 786436
Sparse Core Ops, SparseCore 0:
  192.5 192.0 reduce-scatter.7
  388.8 198.4 reduce-scatter.5
  591.6 211.6 reduce-scatter.9
  806.9 211.3 reduce-scatter.11
where the time goes:
time: 1040 us; the launch traced here: 1030 us
  waiting for transfers between devices  629 us (60%)
  matrix products  141 us (14%)
  local copies, waits for them, and re-layouts  92.7 us (9%)
  blocking collectives  63 us (6%)
  starting transfers between devices  50 us (5%)
  other arithmetic  40.5 us (4%)
  between operations  15.6 us (2%)
    reduce_scatter x1, waiting for transfers between devices, per_device(): lax.psum_scatter(terms[3].astype(jnp.bfloat16), 'pts', scatter_dimension=...  215 us
    reduce_scatter x1, waiting for transfers between devices, per_device(): lax.psum_scatter(terms[4].astype(jnp.bfloat16), 'pts', scatter_dimension=...  214 us
    reduce_scatter x1, waiting for transfers between devices, per_device(): lax.psum_scatter(terms[1].astype(jnp.bfloat16), 'pts', scatter_dimension=...  159 us
    unnamed x1, blocking collectives  63 us
    dot_general x48, matrix products, head_attention(): jnp.dot(head_packed[:, 0], head_packed[:, 1].T, preferred_element_type=jn...  55.6 us
    dot_general x48, matrix products, head_attention(): jnp.dot(attn, head_packed[:, 2], preferred_element_type=jnp.float32)  49.5 us
    all_to_all x2, waiting for transfers between devices, fetch_rows(): lax.all_to_all(outgoing, 'pts', split_axis=0, concat_axis=0, tiled=True)  26.1 us
    dynamic_update_slice x48, other arithmetic, patch_attention(): mixed = lax.map(head_attention, heads_first)  26 us
  transfers between devices with their start and end apart: 10, of which 8 were waited for; matrix products, arithmetic and copies ran while one was open for 16% of the time, Pallas kernels for 0%

commit v1 on v0

v1 whole, which is shorter than its diff:
```python
import functools
import math

import jax
import jax.numpy as jnp
from jax import lax
from jax.experimental import pallas as pl
from jax.experimental.pallas import tpu as pltpu
from jax.sharding import PartitionSpec as P

f32, bf16 = jnp.float32, jnp.bfloat16
MESH = pl.DeviceIdType.MESH
D, HEADS, FF, HD = 256, 8, 1024, 32
N = 512
NX, NZ = 4, 8
PEERS = NX * NZ
SLOT = 32
SLOTS = PEERS * SLOT
WIDE = 1664
SCALE = HD**-0.5
LOG2E = math.log2(math.e)


def nn(a, b):
    return jnp.dot(a, b, preferred_element_type=f32)


def nt(a, b):
    return lax.dot_general(a, b, (((1,), (1,)), ((), ())), preferred_element_type=f32)


def iota(shape, axis):
    return lax.broadcasted_iota(jnp.int32, shape, axis)


def one_hot(condition):
    return jnp.where(condition, 1.0, 0.0).astype(bf16)


def norm_stats(x):
    center = x - jnp.mean(x, axis=0, keepdims=True)
    r = lax.rsqrt(jnp.mean(center * center, axis=0, keepdims=True) + 1e-5)
    return center * r, r


def norm_back(dn, xh, r, gain):
    dxh = dn * gain
    m1 = jnp.mean(dxh, axis=0, keepdims=True)
    m2 = jnp.mean(dxh * xh, axis=0, keepdims=True)
    return r * (dxh - m1 - xh * m2)


def heads_loop(head, per=2):
    def body(i, c):
        for k in range(per):
            head(i * per + k)
        return c

    lax.fori_loop(0, HEADS // per, body, 0)


def forward(x, s, b):
    xh, r = norm_stats(x)
    s.xh1[b] = xh
    s.r1[b] = r
    n1 = (xh * s.gain[2 * b][:, 0:1]).astype(bf16)
    s.n1[b] = n1
    s.qkv[b] = nn(s.qkv_t[b], n1).astype(bf16)
    s.kv[b] = nn(n1.T, s.qkv_w[b][:, D:]).astype(bf16)

    def head(h):
        rows = pl.multiple_of(h * HD, HD)
        keys = s.kv[b, :, :D] * s.mask[pl.ds(h, 1), :].astype(bf16)
        scores = nn(keys, s.qkv[b, :D, :])
        e = jnp.exp2(scores * (SCALE * LOG2E))
        p = (e * (1.0 / jnp.sum(e, axis=0, keepdims=True))).astype(bf16)
        s.attn[b, h] = p
        s.mix[b, pl.ds(rows, HD), :] = nn(s.qkv[b, pl.ds(rows + 2 * D, HD), :], p).astype(bf16)

    heads_loop(head)
    a = x + nn(s.proj_t[b], s.mix[b])
    xh2, r2 = norm_stats(a)
    s.xh2[b] = xh2
    s.r2[b] = r2
    n2 = (xh2 * s.gain[2 * b + 1][:, 0:1]).astype(bf16)
    s.n2[b] = n2
    u = nn(s.exp_t[b], n2)
    cdf = 0.5 + 0.5 * lax.erf(u * (0.5**0.5))
    hid = (u * cdf).astype(bf16)
    s.u[b] = u
    s.cdf[b] = cdf
    s.hid[b] = hid
    return (a + nn(s.con_t[b], hid)).astype(bf16)


def gelu_slope(s, b):
    u = s.u[b]
    s.u[b] = s.cdf[b] + u * (jnp.exp2(u * u * (-0.5 * LOG2E)) * (1 / math.sqrt(2 * math.pi)))


def backward(dy, s, b):
    du = (nn(s.con_w[b], dy).astype(bf16).astype(f32) * s.u[b]).astype(bf16)
    s.du[...] = du
    dn2 = nn(s.exp_w[b], du).astype(bf16).astype(f32)
    s.dn2[...] = dn2
    da = dy.astype(f32) + norm_back(dn2, s.xh2[b], s.r2[b], s.gain[2 * b + 1][:, 0:1])
    dab = da.astype(bf16)
    s.dab[...] = dab
    s.dmix[...] = nn(s.proj_w[b], dab).astype(bf16)

    def head(h):
        rows = pl.multiple_of(h * HD, HD)
        do = s.dmix[pl.ds(rows, HD), :]
        mixed = s.mix[b, pl.ds(rows, HD), :].astype(f32)
        delta = jnp.sum(do.astype(f32) * mixed, axis=0, keepdims=True)
        p = s.attn[b, h]
        values = s.kv[b, :, D:] * s.mask[pl.ds(h, 1), :].astype(bf16)
        ds = (p.astype(f32) * (nn(values, s.dmix[...]) - delta)).astype(bf16)
        query, key = s.qkv[b, pl.ds(rows, HD), :], s.qkv[b, pl.ds(rows + D, HD), :]
        s.dqkv[pl.ds(rows + 2 * D, HD), :] = nt(do, p).astype(bf16)
        s.dqkv[pl.ds(rows + D, HD), :] = (nt(query, ds) * SCALE).astype(bf16)
        s.dqkv[pl.ds(rows, HD), :] = (nn(key, ds) * SCALE).astype(bf16)

    heads_loop(head)
    dn1 = nn(s.qkv_w[b], s.dqkv[...]).astype(bf16).astype(f32)
    s.dn1[...] = dn1
    return (da + norm_back(dn1, s.xh1[b], s.r1[b], s.gain[2 * b][:, 0:1])).astype(bf16)


def weight_grads(dy, s):
    qkv = nt(s.n1[1], s.dqkv[...])
    proj = nt(s.mix[1], s.dab[...])
    first = jnp.concatenate([qkv, proj], axis=1).reshape(PEERS, 8, FF)
    second = nt(s.n2[1], s.du[...]).reshape(PEERS, 8, FF)
    s.grads[:, :, :FF] = jnp.concatenate([first, second], axis=1).astype(bf16)
    contract = nt(s.hid[1], dy).astype(bf16).reshape(PEERS, 32, D)
    s.grads[:, :, FF : FF + D] = contract[:, :16]
    s.grads[:, :, FF + D : FF + 2 * D] = contract[:, 16:]
    g1 = jnp.sum(s.dn1[...] * s.xh1[1], axis=1, keepdims=True)
    g2 = jnp.sum(s.dn2[...] * s.xh2[1], axis=1, keepdims=True)
    lane = iota((D, 128), 1)
    gains = jnp.where(lane == 0, g1, jnp.where(lane == 1, g2, 0.0)).reshape(PEERS, 8, 128)
    s.grads[:, :, FF + 2 * D :] = jnp.concatenate([gains, jnp.zeros_like(gains)], axis=1).astype(bf16)


def plan(order, shift):
    source, local = order // N, order % N
    member = one_hot(source == iota((PEERS, N), 0))
    before = one_hot(iota((N, N), 0) < iota((N, N), 1))
    rank = jnp.sum(member.astype(f32) * nn(member, before), axis=0, keepdims=True).astype(jnp.int32)
    at_slot = one_hot(rank + shift == iota((128, N), 0))
    wanted = local + 1
    high, low = (wanted // 256).astype(f32).astype(bf16), (wanted % 256).astype(f32).astype(bf16)
    asked = nt(member * high, at_slot) * 256.0 + nt(member * low, at_slot)
    return source * SLOT + rank, asked


def pack_matrix(asked, shift):
    at = iota((PEERS, SLOT, 128), 2) == iota((PEERS, SLOT, 128), 1) + shift
    column = jnp.sum(jnp.where(at, asked, 0.0), axis=2, keepdims=True).astype(jnp.int32)
    return one_hot(column == iota((PEERS, SLOT, N), 2) + 1).reshape(SLOTS, N)


class State:
    pass


SCRATCH = dict(
    mask=pltpu.VMEM((HEADS, D), f32),
    gain=pltpu.VMEM((4, D, 128), f32),
    xh1=pltpu.VMEM((2, D, N), f32),
    r1=pltpu.VMEM((2, 1, N), f32),
    xh2=pltpu.VMEM((2, D, N), f32),
    r2=pltpu.VMEM((2, 1, N), f32),
    n1=pltpu.VMEM((2, D, N), bf16),
    n2=pltpu.VMEM((2, D, N), bf16),
    qkv=pltpu.VMEM((2, 3 * D, N), bf16),
    kv=pltpu.VMEM((2, N, 2 * D), bf16),
    attn=pltpu.VMEM((2, HEADS, N, N), bf16),
    mix=pltpu.VMEM((2, D, N), bf16),
    u=pltpu.VMEM((2, FF, N), f32),
    cdf=pltpu.VMEM((2, FF, N), f32),
    hid=pltpu.VMEM((2, FF, N), bf16),
    du=pltpu.VMEM((FF, N), bf16),
    dab=pltpu.VMEM((D, N), bf16),
    dn1=pltpu.VMEM((D, N), f32),
    dn2=pltpu.VMEM((D, N), f32),
    dmix=pltpu.VMEM((D, N), bf16),
    dqkv=pltpu.VMEM((3 * D, N), bf16),
    qkv_t=pltpu.VMEM((2, 3 * D, D), bf16),
    proj_t=pltpu.VMEM((2, D, D), bf16),
    exp_t=pltpu.VMEM((2, FF, D), bf16),
    con_t=pltpu.VMEM((2, D, FF), bf16),
    cot_t=pltpu.VMEM((D, N), bf16),
    pack=pltpu.VMEM((2, SLOTS, N), bf16),
    place=pltpu.VMEM((2, SLOTS, N), bf16),
    ask_out=pltpu.VMEM((PEERS, 1, 128), f32),
    ask_in=pltpu.VMEM((PEERS, 1, 128), f32),
    out=pltpu.VMEM((4, PEERS, SLOT, D), bf16),
    inc=pltpu.VMEM((4, PEERS, SLOT, D), bf16),
    grads=pltpu.VMEM((PEERS, 16, WIDE), bf16),
    grads_x=pltpu.VMEM((NX, NZ, 16, WIDE), bf16),
    part=pltpu.VMEM((NZ, 16, WIDE), bf16),
    grads_z=pltpu.VMEM((NZ, 16, WIDE), bf16),
    ask_send=pltpu.SemaphoreType.DMA((PEERS,)),
    ask_recv=pltpu.SemaphoreType.DMA((PEERS,)),
    row_send=pltpu.SemaphoreType.DMA((4, PEERS)),
    row_recv=pltpu.SemaphoreType.DMA((4, PEERS)),
    x_send=pltpu.SemaphoreType.DMA((NX,)),
    x_recv=pltpu.SemaphoreType.DMA((NX,)),
    z_send=pltpu.SemaphoreType.DMA((NZ,)),
    z_recv=pltpu.SemaphoreType.DMA((NZ,)),
)


def kernel(
    morton_ref,
    hilbert_ref,
    features_ref,
    cotangent_ref,
    gains_ref,
    qkv_ref,
    proj_ref,
    expand_ref,
    contract_ref,
    block_ref,
    feature_ref,
    gain_ref,
    dqkv_ref,
    dproj_ref,
    dexpand_ref,
    dcontract_ref,
    *scratch,
):
    s = State()
    for name, ref in zip(SCRATCH, scratch):
        setattr(s, name, ref)
    s.qkv_w, s.proj_w, s.exp_w, s.con_w = qkv_ref, proj_ref, expand_ref, contract_ref
    me = lax.axis_index("pts")
    my_x, my_z = me // NZ, me % NZ

    def toward(k):
        return (my_x + k // NZ) % NX * NZ + (my_z + k % NZ) % NZ

    def origin(k):
        return (my_x + NX - k // NZ) % NX * NZ + (my_z + NZ - k % NZ) % NZ

    def loop(body):
        def one(k, c):
            body(k)
            return c

        lax.fori_loop(1, PEERS, one, 0)

    def copy(src, dst, send_sem, recv_sem, to):
        return pltpu.make_async_remote_copy(
            src_ref=src,
            dst_ref=dst,
            send_sem=send_sem,
            recv_sem=recv_sem,
            device_id={"pts": to},
            device_id_type=MESH,
        )

    def ask_copy(k, slot):
        to = toward(k)
        return copy(s.ask_out.at[to], s.ask_in.at[slot], s.ask_send.at[k], s.ask_recv.at[k], to)

    def row_copy(e, k, slot):
        to = toward(k)
        return copy(s.out.at[e, to], s.inc.at[e, slot], s.row_send.at[e, k], s.row_recv.at[e, k], to)

    def send_rows(e, rows):
        s.out[e] = rows.astype(bf16).reshape(PEERS, SLOT, D)
        loop(lambda k: row_copy(e, k, me).start())
        s.inc[e, me] = s.out[e, me]

    def received(e):
        loop(lambda k: row_copy(e, k, origin(k)).wait_recv())
        return s.inc[e].reshape(SLOTS, D).T

    barrier = pltpu.get_barrier_semaphore()
    loop(lambda k: pl.semaphore_signal(barrier, inc=1, device_id={"pts": toward(k)}, device_id_type=MESH))

    places = []
    asked = jnp.zeros((PEERS, 128), f32)
    for i, order_ref in enumerate((morton_ref, hilbert_ref)):
        place, wanted = plan(order_ref[...], i * SLOT)
        places.append(place)
        asked = asked + wanted
    for p in range(PEERS):
        s.ask_out[p] = asked[p : p + 1, :]
    pl.semaphore_wait(barrier, PEERS - 1)
    loop(lambda k: ask_copy(k, me).start())
    s.ask_in[me] = s.ask_out[me]

    for i in range(2):
        s.place[i] = one_hot(places[i] == iota((SLOTS, N), 0))
    s.mask[...] = jnp.where(iota((HEADS, D), 1) // HD == iota((HEADS, D), 0), 1.0, 0.0)
    for i in range(4):
        row = gains_ref[i // 2, i % 2 : i % 2 + 1, :].astype(f32)
        s.gain[i] = jnp.broadcast_to(row, (128, D)).T

    def transpose_weights(b):
        s.qkv_t[b] = qkv_ref[b].T
        s.proj_t[b] = proj_ref[b].T
        s.exp_t[b] = expand_ref[b].T
        s.con_t[b] = contract_ref[b].T

    loop(lambda k: ask_copy(k, origin(k)).wait_recv())
    s.pack[0] = pack_matrix(s.ask_in[...], 0)
    send_rows(0, nn(s.pack[0], features_ref[...]))
    transpose_weights(0)
    transpose_weights(1)
    s.pack[1] = pack_matrix(s.ask_in[...], SLOT)
    s.cot_t[...] = cotangent_ref[...].T

    morton_rows = nn(received(0), s.place[0])
    morton_out = forward(morton_rows, s, 0)
    send_rows(1, nt(s.pack[1], morton_out))
    gelu_slope(s, 0)

    hilbert_rows = nn(received(1), s.place[1])
    out = forward(hilbert_rows, s, 1)
    block_ref[...] = out.T
    gelu_slope(s, 1)
    hilbert_grad = backward(s.cot_t[...], s, 1)
    send_rows(2, nt(s.place[1], hilbert_grad))

    weight_grads(s.cot_t[...], s)

    def x_copy(k):
        x = (my_x + k) % NX
        slab = s.grads.at[pl.ds(pl.multiple_of(x * NZ, NZ), NZ)]
        return copy(slab, s.grads_x.at[k], s.x_send.at[k], s.x_recv.at[k], x * NZ + my_z)

    def z_copy(k):
        z = (my_z + k) % NZ
        return copy(s.part.at[z], s.grads_z.at[k], s.z_send.at[k], s.z_recv.at[k], my_x * NZ + z)

    for k in range(1, NX):
        x_copy(k).start()

    morton_grad = nn(received(2), s.pack[1]).astype(bf16)
    morton_row_grad = backward(morton_grad, s, 0)
    send_rows(3, nt(s.place[0], morton_row_grad))

    for k in range(1, NX):
        x_copy(k).wait_recv()
    total = s.grads[pl.ds(pl.multiple_of(my_x * NZ, NZ), NZ)].astype(f32)
    for k in range(1, NX):
        total = total + s.grads_x[k].astype(f32)
    s.part[...] = total.astype(bf16)
    for k in range(1, NZ):
        z_copy(k).start()

    feature_ref[...] = nn(received(3), s.pack[0]).astype(bf16).T

    for k in range(1, NZ):
        z_copy(k).wait_recv()
    total = s.part[my_z].astype(f32)
    for k in range(1, NZ):
        total = total + s.grads_z[k].astype(f32)
    dqkv_ref[...] = total[:8, : 3 * D]
    dproj_ref[...] = total[:8, 3 * D : FF]
    dexpand_ref[...] = total[8:, :FF]
    dcontract_ref[:16, :] = total[:, FF : FF + D]
    dcontract_ref[16:, :] = total[:, FF + D : FF + 2 * D]
    gain_ref[...] = total[:8, FF + 2 * D :].T[:2, :]

    loop(lambda k: ask_copy(k, me).wait_send())
    for e in range(4):
        loop(lambda k: row_copy(e, k, me).wait_send())
    for k in range(1, NX):
        x_copy(k).wait_send()
    for k in range(1, NZ):
        z_copy(k).wait_send()


def per_device(features, morton_order, hilbert_order, cotangent, gains, qkv, proj, expand, contract):
    vmem = pl.BlockSpec(memory_space=pltpu.VMEM)
    shapes = [((N, D), bf16), ((N, D), bf16), ((2, 8), f32), ((8, 3 * D), f32), ((8, D), f32), ((8, FF), f32), ((32, D), f32)]
    return pl.pallas_call(
        kernel,
        out_shape=tuple(jax.ShapeDtypeStruct(*shape) for shape in shapes),
        in_specs=[vmem] * 9,
        out_specs=(vmem,) * 7,
        scratch_shapes=list(SCRATCH.values()),
        compiler_params=pltpu.CompilerParams(
            collective_id=0, has_side_effects=True, vmem_limit_bytes=60 << 20
        ),
    )(morton_order.reshape(1, N), hilbert_order.reshape(1, N), features, cotangent, gains, qkv, proj, expand, contract)


def solution(mesh):
    rows = P(("dp", "pts"), None)
    order = P(("dp", "pts"))
    return jax.shard_map(
        per_device,
        mesh=mesh,
        in_specs=(rows, order, order, rows, P(), P(), P(), P(), P()),
        out_specs=(rows, rows, P("dp", "pts"), rows, rows, rows, rows),
        check_vma=False,
    )
```

time: 1040 us -> 119 us (0.11)
  waiting for transfers between devices: 629 us -> 0 us
  matrix products: 141 us -> 0 us
  Pallas kernels: 0 us -> 112 us
  local copies, waits for them, and re-layouts: 92.7 us -> 5.68 us
  blocking collectives: 63 us -> 0 us
  starting transfers between devices: 50 us -> 0 us
  other arithmetic: 40.5 us -> 0 us
  between operations: 15.6 us -> 0.66 us
    reduce_scatter x4 -> x0, waiting for transfers between devices: 587 us -> none  [the longest x1 215 us: per_device(): lax.psum_scatter(terms[3].astype(jnp.bfloat16), 'pts', scatter_dimension=...]
    dot_general x115 -> x0, matrix products: 141 us -> none  [the longest x48 55.6 us: head_attention(): jnp.dot(head_packed[:, 0], head_packed[:, 1].T, preferred_element_type=jn...]
    pallas_call x0 -> x1, Pallas kernels: none -> 112 us  [per_device(): pl.pallas_call(kernel, out_shape=tuple((jax.ShapeDtypeStruct(*shape) for...]
    unnamed x1 -> x0, blocking collectives: 63 us -> none
    all_to_all x6 -> x0, starting transfers between devices: 49.3 us -> none  [the longest x2 19 us: send_requests(): return lax.all_to_all(asked, 'pts', split_axis=0, concat_axis=0, tiled=True)]
    all_to_all x6 -> x0, waiting for transfers between devices: 41.5 us -> none  [the longest x2 26.1 us: fetch_rows(): lax.all_to_all(outgoing, 'pts', split_axis=0, concat_axis=0, tiled=True)]
    dynamic_update_slice x48 -> x0, other arithmetic: 26 us -> none  [patch_attention(): mixed = lax.map(head_attention, heads_first)]
    scatter x7 -> x0, local copies, waits for them, and re-layouts: 22 us -> none  [the longest x3 11.8 us: return_rows(): landed.at[wanted.reshape(-1)]]
  transfers between devices with their start and end apart: 10 -> 0, of which waited for: 8 -> 0; matrix products, arithmetic and copies ran while one was open for 16% -> 0% of each run, Pallas kernels for 0% -> 0%
where the time goes in v1:
time: 119 us
  Pallas kernels  112 us (94%)
  local copies, waits for them, and re-layouts  5.68 us (5%)
    pallas_call x1, Pallas kernels, per_device(): pl.pallas_call(kernel, out_shape=tuple((jax.ShapeDtypeStruct(*shape) for...  112 us
    unnamed x19, local copies, waits for them, and re-layouts  5.68 us

profile of v1, /device:TPU:22, one launch (start us, length us, event | category | flops | bytes accessed | tf_op | source)
XLA Modules:
  0.0 118.8 jit_solution(9171170987792293088)
XLA Ops:
  0.6 112.5 %shard_map.144 = (bf16[512,256]{1,0:T(8,128)(2,1)}, bf16[512,256]{1,0:T(8,128)(2,1)}, f32[2,8]{1,0:T(2,128)}, f32[8,768]{1,0:T(8,128)}, f32[8,256]{1,0:T(8,128)}, /*index=5*/f32[8,1024]{1,0:T(8,128)}, f32[32,256]{1,0:T(8,128)}) custom-call(s32[1,512]{1,0:T(1,128)} %bitcast.2, s32[1,512]{1,0:T(1,128)} %bitcast.3, bf16[512,256]{1,0:T(8,128)(2,1)} %features_ref.1, ...), custom_call_target="tpu_custom_call" | custom-call | tf_op jit(solution)/shard_map/pallas_call | solution.py:383
  113.1 0.0 copy-start
  113.1 1.7 %copy.23 = bf16[512,256]{1,0:T(8,128)(2,1)} copy(bf16[512,256]{1,0:T(8,128)(2,1)} %get-tuple-element.14) | data formatting | bytes 524288
  114.8 0.0 copy-done
  114.8 0.0 copy-start.5
  114.8 0.0 copy-start.3
  114.8 0.7 copy.24
  115.5 0.0 copy-done.5
  115.5 0.6 copy.25
  116.1 0.0 copy-done.3
  116.1 0.0 copy-start.4
  116.1 0.0 copy-start.2
  116.1 0.6 copy.26
  116.7 0.1 copy-done.4
  116.8 0.6 copy.27
  117.4 0.0 copy-done.2
  117.4 0.0 copy-start.1
  117.4 0.6 copy.28
  118.0 0.2 copy-done.1
  118.2 0.6 copy.29
Async XLA Ops:
  113.1 1.7 %copy-start = (bf16[512,256]{1,0:T(8,128)(2,1)S(1)}, bf16[512,256]{1,0:T(8,128)(2,1)}, u32[]{:S(2)}) copy-start(bf16[512,256]{1,0:T(8,128)(2,1)} %get-tuple-element.15) | copy-start | bytes 786436
  114.8 0.7 copy-start.5
  114.8 1.3 %copy-start.3 = (f32[8,768]{1,0:T(8,128)S(1)}, f32[8,768]{1,0:T(8,128)}, u32[]{:S(2)}) copy-start(f32[8,768]{1,0:T(8,128)} %get-tuple-element.17) | copy-start | bytes 73732
  116.1 0.7 copy-start.4
  116.1 1.3 %copy-start.2 = (f32[8,1024]{1,0:T(8,128)S(1)}, f32[8,1024]{1,0:T(8,128)}, u32[]{:S(2)}) copy-start(f32[8,1024]{1,0:T(8,128)} %get-tuple-element.19) | copy-start | bytes 98308
  117.4 0.8 copy-start.1

commit v2 on v1

v2 whole, which is shorter than its diff:
```python
import functools
import math

import jax
import jax.numpy as jnp
from jax import lax
from jax.experimental import pallas as pl
from jax.experimental.pallas import tpu as pltpu
from jax.sharding import PartitionSpec as P

f32, bf16 = jnp.float32, jnp.bfloat16
MESH = pl.DeviceIdType.MESH
D, HEADS, FF, HD = 256, 8, 1024, 32
N = 512
NX, NZ = 4, 8
PEERS = NX * NZ
SLOT = 32
SLOTS = PEERS * SLOT
WIDE = (1024, 640)
SCALE = HD**-0.5
LOG2E = math.log2(math.e)


def nn(a, b):
    return jnp.dot(a, b, preferred_element_type=f32)


def nt(a, b):
    return lax.dot_general(a, b, (((1,), (1,)), ((), ())), preferred_element_type=f32)


def iota(shape, axis):
    return lax.broadcasted_iota(jnp.int32, shape, axis)


def one_hot(condition):
    return jnp.where(condition, 1.0, 0.0).astype(bf16)


def norm_stats(x):
    center = x - jnp.mean(x, axis=0, keepdims=True)
    r = lax.rsqrt(jnp.mean(center * center, axis=0, keepdims=True) + 1e-5)
    return center * r, r


def norm_back(dn, xh, r, gain):
    dxh = dn * gain
    m1 = jnp.mean(dxh, axis=0, keepdims=True)
    m2 = jnp.mean(dxh * xh, axis=0, keepdims=True)
    return r * (dxh - m1 - xh * m2)


def heads_loop(head, per=4):
    def body(i, c):
        for k in range(per):
            head(i * per + k)
        return c

    lax.fori_loop(0, HEADS // per, body, 0)


def forward(x, s, b):
    xh, r = norm_stats(x)
    s.xh1[b] = xh
    s.r1[b] = r
    n1 = (xh * s.gain[2 * b][:, 0:1]).astype(bf16)
    s.n1[b] = n1
    s.qkv[b] = nn(s.qkv_t[b], n1).astype(bf16)
    s.kv[b] = nn(n1.T, s.qkv_w[b][:, D:]).astype(bf16)

    def head(h):
        rows = pl.multiple_of(h * HD, HD)
        keys = s.kv[b, :, :D] * s.mask[pl.ds(h, 1), :].astype(bf16)
        scores = nn(keys, s.qkv[b, :D, :])
        e = jnp.exp2(scores * (SCALE * LOG2E))
        p = (e * (1.0 / jnp.sum(e, axis=0, keepdims=True))).astype(bf16)
        s.attn[b, h] = p
        s.mix[b, pl.ds(rows, HD), :] = nn(s.qkv[b, pl.ds(rows + 2 * D, HD), :], p).astype(bf16)

    heads_loop(head)
    a = x + nn(s.proj_t[b], s.mix[b])
    xh2, r2 = norm_stats(a)
    s.xh2[b] = xh2
    s.r2[b] = r2
    n2 = (xh2 * s.gain[2 * b + 1][:, 0:1]).astype(bf16)
    s.n2[b] = n2
    u = nn(s.exp_t[b], n2)
    cdf = 0.5 + 0.5 * lax.erf(u * (0.5**0.5))
    hid = (u * cdf).astype(bf16)
    s.u[b] = u
    s.cdf[b] = cdf
    s.hid[b] = hid
    return (a + nn(s.con_t[b], hid)).astype(bf16)


def gelu_slope(s, b):
    u = s.u[b]
    s.u[b] = s.cdf[b] + u * (jnp.exp2(u * u * (-0.5 * LOG2E)) * (1 / math.sqrt(2 * math.pi)))


def fold(grad):
    half = grad.shape[1] // 2
    left, right = grad[:, :half].reshape(PEERS, 8, half), grad[:, half:].reshape(PEERS, 8, half)
    return jnp.concatenate([left, right], axis=1).astype(bf16)


def mlp_grads(dy, s):
    s.grads_a[:, :, :N] = fold(nt(s.n2[1], s.du[...]))
    contract = nt(s.hid[1], dy).astype(bf16).reshape(PEERS, 32, D)
    s.grads_a[:, :, N : N + D] = contract[:, :16]
    s.grads_a[:, :, N + D :] = contract[:, 16:]


def attention_grads(s):
    s.grads_b[:, :, :N] = fold(jnp.concatenate([nt(s.n1[1], s.dqkv[...]), nt(s.mix[1], s.dab[...])], axis=1))
    g1 = jnp.sum(s.dn1[...] * s.xh1[1], axis=1, keepdims=True)
    g2 = jnp.sum(s.dn2[...] * s.xh2[1], axis=1, keepdims=True)
    lane = iota((D, 256), 1)
    s.grads_b[:, :, N:] = fold(jnp.where(lane == 0, g1, jnp.where(lane == 1, g2, 0.0)))


def backward(dy, s, b, after_mlp=None):
    du = (nn(s.con_w[b], dy).astype(bf16).astype(f32) * s.u[b]).astype(bf16)
    s.du[...] = du
    if after_mlp is not None:
        after_mlp()
    dn2 = nn(s.exp_w[b], s.du[...]).astype(bf16).astype(f32)
    s.dn2[...] = dn2
    da = dy.astype(f32) + norm_back(dn2, s.xh2[b], s.r2[b], s.gain[2 * b + 1][:, 0:1])
    s.da[...] = da
    dab = da.astype(bf16)
    s.dab[...] = dab
    s.dmix[...] = nn(s.proj_w[b], dab).astype(bf16)

    def head(h):
        rows = pl.multiple_of(h * HD, HD)
        do = s.dmix[pl.ds(rows, HD), :]
        mixed = s.mix[b, pl.ds(rows, HD), :].astype(f32)
        delta = jnp.sum(do.astype(f32) * mixed, axis=0, keepdims=True)
        p = s.attn[b, h]
        values = s.kv[b, :, D:] * s.mask[pl.ds(h, 1), :].astype(bf16)
        ds = (p.astype(f32) * (nn(values, s.dmix[...]) - delta)).astype(bf16)
        query, key = s.qkv[b, pl.ds(rows, HD), :], s.qkv[b, pl.ds(rows + D, HD), :]
        s.dqkv[pl.ds(rows + 2 * D, HD), :] = nt(do, p).astype(bf16)
        s.dqkv[pl.ds(rows + D, HD), :] = (nt(query, ds) * SCALE).astype(bf16)
        s.dqkv[pl.ds(rows, HD), :] = (nn(key, ds) * SCALE).astype(bf16)

    heads_loop(head)
    dn1 = nn(s.qkv_w[b], s.dqkv[...]).astype(bf16).astype(f32)
    s.dn1[...] = dn1
    return (s.da[...] + norm_back(dn1, s.xh1[b], s.r1[b], s.gain[2 * b][:, 0:1])).astype(bf16)


def plan(order, shift):
    source, local = order >> 9, order & (N - 1)
    member = one_hot(source == iota((PEERS, N), 0))
    before = one_hot(iota((N, N), 0) < iota((N, N), 1))
    rank = jnp.sum(member.astype(f32) * nn(member, before), axis=0, keepdims=True).astype(jnp.int32)
    at_slot = one_hot(rank + shift == iota((128, N), 0))
    wanted = local + 1
    high, low = (wanted >> 8).astype(f32).astype(bf16), (wanted & 255).astype(f32).astype(bf16)
    asked = nt(member * high, at_slot) * 256.0 + nt(member * low, at_slot)
    return source * SLOT + rank, asked


def pack_matrix(asked, shift):
    at = iota((PEERS, SLOT, 128), 2) == iota((PEERS, SLOT, 128), 1) + shift
    column = jnp.sum(jnp.where(at, asked, 0.0), axis=2, keepdims=True).astype(jnp.int32)
    return one_hot(column == iota((PEERS, SLOT, N), 2) + 1).reshape(SLOTS, N)


class State:
    pass


SCRATCH = dict(
    mask=pltpu.VMEM((HEADS, D), f32),
    gain=pltpu.VMEM((4, D, 128), f32),
    xh1=pltpu.VMEM((2, D, N), f32),
    r1=pltpu.VMEM((2, 1, N), f32),
    xh2=pltpu.VMEM((2, D, N), f32),
    r2=pltpu.VMEM((2, 1, N), f32),
    n1=pltpu.VMEM((2, D, N), bf16),
    n2=pltpu.VMEM((2, D, N), bf16),
    qkv=pltpu.VMEM((2, 3 * D, N), bf16),
    kv=pltpu.VMEM((2, N, 2 * D), bf16),
    attn=pltpu.VMEM((2, HEADS, N, N), bf16),
    mix=pltpu.VMEM((2, D, N), bf16),
    u=pltpu.VMEM((2, FF, N), f32),
    cdf=pltpu.VMEM((2, FF, N), f32),
    hid=pltpu.VMEM((2, FF, N), bf16),
    du=pltpu.VMEM((FF, N), bf16),
    dab=pltpu.VMEM((D, N), bf16),
    dn1=pltpu.VMEM((D, N), f32),
    dn2=pltpu.VMEM((D, N), f32),
    dmix=pltpu.VMEM((D, N), bf16),
    dqkv=pltpu.VMEM((3 * D, N), bf16),
    qkv_t=pltpu.VMEM((2, 3 * D, D), bf16),
    proj_t=pltpu.VMEM((2, D, D), bf16),
    exp_t=pltpu.VMEM((2, FF, D), bf16),
    con_t=pltpu.VMEM((2, D, FF), bf16),
    cot_t=pltpu.VMEM((D, N), bf16),
    out_t=pltpu.VMEM((D, N), bf16),
    rows_t=pltpu.VMEM((D, N), bf16),
    grad_t=pltpu.VMEM((D, N), bf16),
    orders=pltpu.VMEM((2, 1, N), jnp.int32),
    gains=pltpu.VMEM((2, 2, D), bf16),
    pack=pltpu.VMEM((2, SLOTS, N), bf16),
    place=pltpu.VMEM((2, SLOTS, N), bf16),
    ask_out=pltpu.VMEM((PEERS, 1, 128), f32),
    ask_in=pltpu.VMEM((PEERS, 1, 128), f32),
    out=pltpu.VMEM((4, PEERS, SLOT, D), bf16),
    inc=pltpu.VMEM((4, PEERS, SLOT, D), bf16),
    da=pltpu.VMEM((D, N), f32),
    qkv_w=pltpu.VMEM((2, D, 3 * D), bf16),
    proj_w=pltpu.VMEM((2, D, D), bf16),
    exp_w=pltpu.VMEM((2, D, FF), bf16),
    con_w=pltpu.VMEM((2, FF, D), bf16),
    rows_in=pltpu.VMEM((N, D), bf16),
    cot=pltpu.VMEM((N, D), bf16),
    grads_a=pltpu.VMEM((PEERS, 16, WIDE[0]), bf16),
    grads_b=pltpu.VMEM((PEERS, 16, WIDE[1]), bf16),
    from_x_a=pltpu.VMEM((NX, NZ, 16, WIDE[0]), bf16),
    from_x_b=pltpu.VMEM((NX, NZ, 16, WIDE[1]), bf16),
    part_a=pltpu.VMEM((NZ, 16, WIDE[0]), bf16),
    part_b=pltpu.VMEM((NZ, 16, WIDE[1]), bf16),
    from_z_a=pltpu.VMEM((NZ, 16, WIDE[0]), bf16),
    from_z_b=pltpu.VMEM((NZ, 16, WIDE[1]), bf16),
    load=pltpu.SemaphoreType.DMA((9,)),
    ask_send=pltpu.SemaphoreType.DMA((PEERS,)),
    ask_recv=pltpu.SemaphoreType.DMA((PEERS,)),
    row_send=pltpu.SemaphoreType.DMA((4, PEERS)),
    row_recv=pltpu.SemaphoreType.DMA((4, PEERS)),
    x_send=pltpu.SemaphoreType.DMA((2, NX)),
    x_recv=pltpu.SemaphoreType.DMA((2, NX)),
    z_send=pltpu.SemaphoreType.DMA((2, NZ)),
    z_recv=pltpu.SemaphoreType.DMA((2, NZ)),
)


def kernel(
    morton_ref,
    hilbert_ref,
    features_ref,
    cotangent_ref,
    gains_ref,
    qkv_ref,
    proj_ref,
    expand_ref,
    contract_ref,
    block_ref,
    feature_ref,
    gain_ref,
    dqkv_ref,
    dproj_ref,
    dexpand_ref,
    dcontract_ref,
    *scratch,
):
    s = State()
    for name, ref in zip(SCRATCH, scratch):
        setattr(s, name, ref)
    me = lax.axis_index("pts")
    my_x, my_z = me // NZ, me % NZ

    def toward(k):
        return lax.rem(my_x + k // NZ, NX) * NZ + lax.rem(my_z + k % NZ, NZ)

    def origin(k):
        return toward((NX - k // NZ) % NX * NZ + (NZ - k % NZ) % NZ)

    def loop(body, order=range(1, PEERS)):
        for k in order:
            body(k)

    def copy(src, dst, send_sem, recv_sem, to):
        return pltpu.make_async_remote_copy(
            src_ref=src,
            dst_ref=dst,
            send_sem=send_sem,
            recv_sem=recv_sem,
            device_id={"pts": to},
            device_id_type=MESH,
        )

    def ask_copy(k, slot):
        to = toward(k)
        return copy(s.ask_out.at[to], s.ask_in.at[slot], s.ask_send.at[k], s.ask_recv.at[k], to)

    def row_copy(e, k, slot):
        to = toward(k)
        return copy(s.out.at[e, to], s.inc.at[e, slot], s.row_send.at[e, k], s.row_recv.at[e, k], to)

    def send_rows(e, matrix, pack):
        for dx in range(NX):
            first = pl.multiple_of(lax.rem(my_x + dx, NX) * NZ, NZ)
            rows = pack(matrix[pl.ds(pl.multiple_of(first * SLOT, SLOT), NZ * SLOT), :])
            s.out[e, pl.ds(first, NZ)] = rows.astype(bf16).reshape(NZ, SLOT, D)
            for k in range(max(dx * NZ, 1), (dx + 1) * NZ):
                row_copy(e, k, me).start()
        s.inc[e, me] = s.out[e, me]

    def received(e, matrix):
        total = None
        for dx in range(NX):
            for k in range(max(dx * NZ, 1), (dx + 1) * NZ):
                row_copy(e, k, origin(k)).wait_recv()
            first = pl.multiple_of(lax.rem(my_x + (NX - dx) % NX, NX) * NZ, NZ)
            rows = s.inc[e, pl.ds(first, NZ)].reshape(NZ * SLOT, D).T
            term = nn(rows, matrix[pl.ds(pl.multiple_of(first * SLOT, SLOT), NZ * SLOT), :])
            total = term if total is None else total + term
        return total

    barrier = pltpu.get_barrier_semaphore()
    loop(lambda k: pl.semaphore_signal(barrier, inc=1, device_id={"pts": toward(k)}, device_id_type=MESH))

    loads = (
        (morton_ref, s.orders.at[0]),
        (hilbert_ref, s.orders.at[1]),
        (features_ref, s.rows_in),
        (gains_ref, s.gains),
        (cotangent_ref, s.cot),
        (qkv_ref, s.qkv_w),
        (proj_ref, s.proj_w),
        (expand_ref, s.exp_w),
        (contract_ref, s.con_w),
    )
    loads = [pltpu.make_async_copy(src, dst, s.load.at[i]) for i, (src, dst) in enumerate(loads)]
    for one in loads:
        one.start()

    places = []
    asked = jnp.zeros((PEERS, 128), f32)
    for i in range(2):
        loads[i].wait()
        place, wanted = plan(s.orders[i], i * SLOT)
        places.append(place)
        asked = asked + wanted
    for p in range(PEERS):
        s.ask_out[p] = asked[p : p + 1, :]
    pl.semaphore_wait(barrier, PEERS - 1)
    loop(lambda k: ask_copy(k, me).start())
    s.ask_in[me] = s.ask_out[me]

    for i in range(2):
        s.place[i] = one_hot(places[i] == iota((SLOTS, N), 0))
    s.mask[...] = jnp.where(iota((HEADS, D), 1) // HD == iota((HEADS, D), 0), 1.0, 0.0)
    loads[3].wait()
    for i in range(4):
        row = s.gains[i // 2, i % 2 : i % 2 + 1, :].astype(f32)
        s.gain[i] = jnp.broadcast_to(row, (128, D)).T

    loop(lambda k: ask_copy(k, origin(k)).wait_recv())
    s.pack[0] = pack_matrix(s.ask_in[...], 0)
    loads[2].wait()
    send_rows(0, s.pack.at[0], lambda m: nn(m, s.rows_in[...]))
    for one in loads[4:]:
        one.wait()
    for b in range(2):
        s.qkv_t[b] = s.qkv_w[b].T
        s.proj_t[b] = s.proj_w[b].T
        s.exp_t[b] = s.exp_w[b].T
        s.con_t[b] = s.con_w[b].T
    s.pack[1] = pack_matrix(s.ask_in[...], SLOT)
    s.cot_t[...] = s.cot[...].T

    morton_rows = received(0, s.place.at[0])
    s.rows_t[...] = forward(morton_rows, s, 0)
    send_rows(1, s.pack.at[1], lambda m: nt(m, s.rows_t[...]))
    gelu_slope(s, 0)

    hilbert_rows = received(1, s.place.at[1])
    s.out_t[...] = forward(hilbert_rows, s, 1)
    gelu_slope(s, 1)

    grads, from_x = (s.grads_a, s.grads_b), (s.from_x_a, s.from_x_b)
    part, from_z = (s.part_a, s.part_b), (s.from_z_a, s.from_z_b)

    def x_copy(i, k):
        x = (my_x + k) % NX
        slab = grads[i].at[pl.ds(pl.multiple_of(x * NZ, NZ), NZ)]
        return copy(slab, from_x[i].at[k], s.x_send.at[i, k], s.x_recv.at[i, k], x * NZ + my_z)

    def z_copy(i, k):
        z = (my_z + k) % NZ
        return copy(part[i].at[z], from_z[i].at[k], s.z_send.at[i, k], s.z_recv.at[i, k], my_x * NZ + z)

    def along_x(i):
        for k in range(1, NX):
            x_copy(i, k).start()

    def along_z(i):
        for k in range(1, NX):
            x_copy(i, k).wait_recv()
        total = grads[i][pl.ds(pl.multiple_of(my_x * NZ, NZ), NZ)].astype(f32)
        for k in range(1, NX):
            total = total + from_x[i][k].astype(f32)
        part[i][...] = total.astype(bf16)
        for k in range(1, NZ):
            z_copy(i, k).start()

    def summed(i):
        for k in range(1, NZ):
            z_copy(i, k).wait_recv()
        total = part[i][my_z].astype(f32)
        for k in range(1, NZ):
            total = total + from_z[i][k].astype(f32)
        return total

    def send_mlp_grads():
        mlp_grads(s.cot_t[...], s)
        along_x(0)

    s.rows_t[...] = backward(s.cot_t[...], s, 1, send_mlp_grads)
    send_rows(2, s.place.at[1], lambda m: nt(m, s.rows_t[...]))
    block_ref[...] = s.out_t[...].T
    attention_grads(s)

    s.grad_t[...] = received(2, s.pack.at[1]).astype(bf16)
    along_x(1)
    along_z(0)
    s.rows_t[...] = backward(s.grad_t[...], s, 0)
    send_rows(3, s.place.at[0], lambda m: nt(m, s.rows_t[...]))
    along_z(1)

    feature_ref[...] = received(3, s.pack.at[0]).astype(bf16).T
    total = summed(0)
    dexpand_ref[:, :N] = total[:8, :N]
    dexpand_ref[:, N:] = total[8:, :N]
    dcontract_ref[:16, :] = total[:, N : N + D]
    dcontract_ref[16:, :] = total[:, N + D :]
    total = summed(1)
    dqkv_ref[:, :N] = total[:8, :N]
    dqkv_ref[:, N:] = total[8:, :D]
    dproj_ref[...] = total[8:, D:N]
    gain_ref[...] = total[:8, N:].T[:2, :]

    loop(lambda k: ask_copy(k, me).wait_send())
    for e in range(4):
        loop(lambda k: row_copy(e, k, me).wait_send())
    for i in range(2):
        for k in range(1, NX):
            x_copy(i, k).wait_send()
        for k in range(1, NZ):
            z_copy(i, k).wait_send()


def hand_on(*refs):
    for source, target in zip(refs[:7], refs[7:]):
        target[...] = source[...]


def per_device(features, morton_order, hilbert_order, cotangent, gains, qkv, proj, expand, contract):
    vmem, hbm = pl.BlockSpec(memory_space=pltpu.VMEM), pl.BlockSpec(memory_space=pl.ANY)
    shapes = [((N, D), bf16), ((N, D), bf16), ((2, 8), f32), ((8, 3 * D), f32), ((8, D), f32), ((8, FF), f32), ((32, D), f32)]
    shapes = tuple(jax.ShapeDtypeStruct(*shape) for shape in shapes)
    results = pl.pallas_call(
        kernel,
        out_shape=shapes,
        in_specs=[hbm] * 9,
        out_specs=(vmem,) * 7,
        scratch_shapes=list(SCRATCH.values()),
        compiler_params=pltpu.CompilerParams(
            collective_id=0, has_side_effects=True, vmem_limit_bytes=60 << 20
        ),
    )(morton_order.reshape(1, N), hilbert_order.reshape(1, N), features, cotangent, gains, qkv, proj, expand, contract)
    return pl.pallas_call(
        hand_on,
        out_shape=shapes,
        in_specs=[vmem] * 7,
        out_specs=(vmem,) * 7,
    )(*results)


def solution(mesh):
    rows = P(("dp", "pts"), None)
    order = P(("dp", "pts"))
    return jax.shard_map(
        per_device,
        mesh=mesh,
        in_specs=(rows, order, order, rows, P(), P(), P(), P(), P()),
        out_specs=(rows, rows, P("dp", "pts"), rows, rows, rows, rows),
        check_vma=False,
    )
```

time: 119 us -> 106 us (0.89); the launches traced: 119 us -> 104 us
  Pallas kernels: 112 us -> 103 us
  local copies, waits for them, and re-layouts: 5.68 us -> 0 us
    pallas_call x1 -> x2, Pallas kernels: 112 us -> 103 us  [the longest x1 101 us: per_device(): pl.pallas_call(kernel, out_shape=shapes, in_specs=[hbm] * 9, out_specs=(v...]
    unnamed x19 -> x0, local copies, waits for them, and re-layouts: 5.68 us -> none
where the time goes in v2:
time: 106 us; the launch traced here: 104 us
  Pallas kernels  103 us (97%)
    pallas_call x1, Pallas kernels, per_device(): pl.pallas_call(kernel, out_shape=shapes, in_specs=[hbm] * 9, out_specs=(v...  101 us

profile of v2, /device:TPU:22, one launch (start us, length us, event | category | flops | bytes accessed | tf_op | source)
XLA Modules:
  0.0 103.9 jit_solution(16381198416828080759)
XLA Ops:
  0.6 101.4 %shard_map.144 = (bf16[512,256]{1,0:T(8,128)(2,1)}, bf16[512,256]{1,0:T(8,128)(2,1)}, f32[2,8]{1,0:T(2,128)}, f32[8,768]{1,0:T(8,128)}, f32[8,256]{1,0:T(8,128)}, /*index=5*/f32[8,1024]{1,0:T(8,128)}, f32[32,256]{1,0:T(8,128)}) custom-call(s32[1,512]{1,0:T(1,128)} %bitcast.2, s32[1,512]{1,0:T(1,128)} %bitcast.3, bf16[512,256]{1,0:T(8,128)(2,1)} %features_ref.1, ...), custom_call_target="tpu_custom_call" | custom-call | tf_op jit(solution)/shard_map/pallas_call | solution.py:457
  102.0 1.9 %shard_map.145 = (bf16[512,256]{1,0:T(8,128)(2,1)}, bf16[512,256]{1,0:T(8,128)(2,1)}, f32[2,8]{1,0:T(2,128)}, f32[8,768]{1,0:T(8,128)}, f32[8,256]{1,0:T(8,128)}, /*index=5*/f32[8,1024]{1,0:T(8,128)}, f32[32,256]{1,0:T(8,128)}) custom-call(bf16[512,256]{1,0:T(8,128)(2,1)} %get-tuple-element.14.refs_0_, bf16[512,256]{1,0:T(8,128)(2,1)} %get-tuple-element.15.refs_1_, ...), custom_call_target="tpu_custom_call" | custom-call | tf_op jit(solution)/shard_map/pallas_call | solution.py:467

commit v3 on v2

--- a/solution.py
+++ b/solution.py
@@ -17,6 +17,8 @@
 SLOT = 32
 SLOTS = PEERS * SLOT
 WIDE = (1024, 640)
+X_ORDER, Z_ORDER = (2, 1, 3, 0), (4, 3, 5, 2, 6, 1, 7, 0)
+GROUPS = [[dx * NZ + dz for dz in Z_ORDER if dx or dz] for dx in X_ORDER]
 SCALE = HD**-0.5
 LOG2E = math.log2(math.e)
 
@@ -269,9 +271,10 @@
     def origin(k):
         return toward((NX - k // NZ) % NX * NZ + (NZ - k % NZ) % NZ)
 
-    def loop(body, order=range(1, PEERS)):
-        for k in order:
-            body(k)
+    def loop(body):
+        for group in GROUPS:
+            for k in group:
+                body(k)
 
     def copy(src, dst, send_sem, recv_sem, to):
         return pltpu.make_async_remote_copy(
@@ -292,18 +295,21 @@
         return copy(s.out.at[e, to], s.inc.at[e, slot], s.row_send.at[e, k], s.row_recv.at[e, k], to)
 
     def send_rows(e, matrix, pack):
-        for dx in range(NX):
+        for dx, group in zip(X_ORDER, GROUPS):
             first = pl.multiple_of(lax.rem(my_x + dx, NX) * NZ, NZ)
             rows = pack(matrix[pl.ds(pl.multiple_of(first * SLOT, SLOT), NZ * SLOT), :])
             s.out[e, pl.ds(first, NZ)] = rows.astype(bf16).reshape(NZ, SLOT, D)
-            for k in range(max(dx * NZ, 1), (dx + 1) * NZ):
+            for k in group:
                 row_copy(e, k, me).start()
         s.inc[e, me] = s.out[e, me]
 
+    def sent(e):
+        loop(lambda k: row_copy(e, k, me).wait_send())
+
     def received(e, matrix):
         total = None
-        for dx in range(NX):
-            for k in range(max(dx * NZ, 1), (dx + 1) * NZ):
+        for dx, group in zip(X_ORDER, GROUPS):
+            for k in group:
                 row_copy(e, k, origin(k)).wait_recv()
             first = pl.multiple_of(lax.rem(my_x + (NX - dx) % NX, NX) * NZ, NZ)
             rows = s.inc[e, pl.ds(first, NZ)].reshape(NZ * SLOT, D).T
@@ -363,11 +369,13 @@
         s.con_t[b] = s.con_w[b].T
     s.pack[1] = pack_matrix(s.ask_in[...], SLOT)
     s.cot_t[...] = s.cot[...].T
+    loop(lambda k: ask_copy(k, me).wait_send())
 
     morton_rows = received(0, s.place.at[0])
     s.rows_t[...] = forward(morton_rows, s, 0)
     send_rows(1, s.pack.at[1], lambda m: nt(m, s.rows_t[...]))
     gelu_slope(s, 0)
+    sent(0)
 
     hilbert_rows = received(1, s.place.at[1])
     s.out_t[...] = forward(hilbert_rows, s, 1)
@@ -415,6 +423,7 @@
     send_rows(2, s.place.at[1], lambda m: nt(m, s.rows_t[...]))
     block_ref[...] = s.out_t[...].T
     attention_grads(s)
+    sent(1)
 
     s.grad_t[...] = received(2, s.pack.at[1]).astype(bf16)
     along_x(1)
@@ -422,6 +431,7 @@
     s.rows_t[...] = backward(s.grad_t[...], s, 0)
     send_rows(3, s.place.at[0], lambda m: nt(m, s.rows_t[...]))
     along_z(1)
+    sent(2)
 
     feature_ref[...] = received(3, s.pack.at[0]).astype(bf16).T
     total = summed(0)
@@ -435,9 +445,7 @@
     dproj_ref[...] = total[8:, D:N]
     gain_ref[...] = total[:8, N:].T[:2, :]
 
-    loop(lambda k: ask_copy(k, me).wait_send())
-    for e in range(4):
-        loop(lambda k: row_copy(e, k, me).wait_send())
+    sent(3)
     for i in range(2):
         for k in range(1, NX):
             x_copy(i, k).wait_send()

time: 106 us -> 101 us (0.953); the launches traced: 104 us -> 100 us
  Pallas kernels: 103 us -> 99.5 us
    pallas_call x1, Pallas kernels: 101 us -> 97.6 us  [per_device(): pl.pallas_call(kernel, out_shape=shapes, in_specs=[hbm] * 9, out_specs=(v...]
where the time goes in v3:
time: 101 us; the launch traced here: 100 us
  Pallas kernels  99.5 us (99%)
    pallas_call x1, Pallas kernels, per_device(): pl.pallas_call(kernel, out_shape=shapes, in_specs=[hbm] * 9, out_specs=(v...  97.6 us

profile of v3, /device:TPU:22, one launch (start us, length us, event | category | flops | bytes accessed | tf_op | source)
XLA Modules:
  0.0 100.2 jit_solution(14364681918815036334)
XLA Ops:
  0.6 97.6 %shard_map.144 = (bf16[512,256]{1,0:T(8,128)(2,1)}, bf16[512,256]{1,0:T(8,128)(2,1)}, f32[2,8]{1,0:T(2,128)}, f32[8,768]{1,0:T(8,128)}, f32[8,256]{1,0:T(8,128)}, /*index=5*/f32[8,1024]{1,0:T(8,128)}, f32[32,256]{1,0:T(8,128)}) custom-call(s32[1,512]{1,0:T(1,128)} %bitcast.2, s32[1,512]{1,0:T(1,128)} %bitcast.3, bf16[512,256]{1,0:T(8,128)(2,1)} %features_ref.1, ...), custom_call_target="tpu_custom_call" | custom-call | tf_op jit(solution)/shard_map/pallas_call | solution.py:465
  98.3 1.9 %shard_map.145 = (bf16[512,256]{1,0:T(8,128)(2,1)}, bf16[512,256]{1,0:T(8,128)(2,1)}, f32[2,8]{1,0:T(2,128)}, f32[8,768]{1,0:T(8,128)}, f32[8,256]{1,0:T(8,128)}, /*index=5*/f32[8,1024]{1,0:T(8,128)}, f32[32,256]{1,0:T(8,128)}) custom-call(bf16[512,256]{1,0:T(8,128)(2,1)} %get-tuple-element.14.refs_0_, bf16[512,256]{1,0:T(8,128)(2,1)} %get-tuple-element.15.refs_1_, ...), custom_call_target="tpu_custom_call" | custom-call | tf_op jit(solution)/shard_map/pallas_call | solution.py:475

commit v4 on v3

--- a/solution.py
+++ b/solution.py
@@ -89,15 +89,17 @@
     u = nn(s.exp_t[b], n2)
     cdf = 0.5 + 0.5 * lax.erf(u * (0.5**0.5))
     hid = (u * cdf).astype(bf16)
-    s.u[b] = u
-    s.cdf[b] = cdf
     s.hid[b] = hid
-    return (a + nn(s.con_t[b], hid)).astype(bf16)
-
-
-def gelu_slope(s, b):
-    u = s.u[b]
-    s.u[b] = s.cdf[b] + u * (jnp.exp2(u * u * (-0.5 * LOG2E)) * (1 / math.sqrt(2 * math.pi)))
+    if b == 0:
+        s.u[...] = u
+        s.cdf[...] = cdf
+        return (a + nn(s.con_t[b], hid)).astype(bf16)
+    s.du[...] = (s.dhid[...].astype(f32) * gelu_slope(u, cdf)).astype(bf16)
+    s.after[...] = a
+
+
+def gelu_slope(u, cdf):
+    return cdf + u * (jnp.exp2(u * u * (-0.5 * LOG2E)) * (1 / math.sqrt(2 * math.pi)))
 
 
 def fold(grad):
@@ -122,8 +124,8 @@
 
 
 def backward(dy, s, b, after_mlp=None):
-    du = (nn(s.con_w[b], dy).astype(bf16).astype(f32) * s.u[b]).astype(bf16)
-    s.du[...] = du
+    if b == 0:
+        s.du[...] = (nn(s.con_w[b], dy).astype(bf16).astype(f32) * s.u[...]).astype(bf16)
     if after_mlp is not None:
         after_mlp()
     dn2 = nn(s.exp_w[b], s.du[...]).astype(bf16).astype(f32)
@@ -188,8 +190,10 @@
     kv=pltpu.VMEM((2, N, 2 * D), bf16),
     attn=pltpu.VMEM((2, HEADS, N, N), bf16),
     mix=pltpu.VMEM((2, D, N), bf16),
-    u=pltpu.VMEM((2, FF, N), f32),
-    cdf=pltpu.VMEM((2, FF, N), f32),
+    u=pltpu.VMEM((FF, N), f32),
+    cdf=pltpu.VMEM((FF, N), f32),
+    after=pltpu.VMEM((D, N), f32),
+    dhid=pltpu.VMEM((FF, N), bf16),
     hid=pltpu.VMEM((2, FF, N), bf16),
     du=pltpu.VMEM((FF, N), bf16),
     dab=pltpu.VMEM((D, N), bf16),
@@ -202,7 +206,6 @@
     exp_t=pltpu.VMEM((2, FF, D), bf16),
     con_t=pltpu.VMEM((2, D, FF), bf16),
     cot_t=pltpu.VMEM((D, N), bf16),
-    out_t=pltpu.VMEM((D, N), bf16),
     rows_t=pltpu.VMEM((D, N), bf16),
     grad_t=pltpu.VMEM((D, N), bf16),
     orders=pltpu.VMEM((2, 1, N), jnp.int32),
@@ -374,12 +377,12 @@
     morton_rows = received(0, s.place.at[0])
     s.rows_t[...] = forward(morton_rows, s, 0)
     send_rows(1, s.pack.at[1], lambda m: nt(m, s.rows_t[...]))
-    gelu_slope(s, 0)
+    s.u[...] = gelu_slope(s.u[...], s.cdf[...])
+    s.dhid[...] = nn(s.con_w[1], s.cot_t[...]).astype(bf16)
     sent(0)
 
     hilbert_rows = received(1, s.place.at[1])
-    s.out_t[...] = forward(hilbert_rows, s, 1)
-    gelu_slope(s, 1)
+    forward(hilbert_rows, s, 1)
 
     grads, from_x = (s.grads_a, s.grads_b), (s.from_x_a, s.from_x_b)
     part, from_z = (s.part_a, s.part_b), (s.from_z_a, s.from_z_b)
@@ -421,7 +424,7 @@
 
     s.rows_t[...] = backward(s.cot_t[...], s, 1, send_mlp_grads)
     send_rows(2, s.place.at[1], lambda m: nt(m, s.rows_t[...]))
-    block_ref[...] = s.out_t[...].T
+    block_ref[...] = (s.after[...] + nn(s.con_t[1], s.hid[1])).astype(bf16).T
     attention_grads(s)
     sent(1)
 

time: 101 us -> 101 us (level)
  no operation moved by 1% of the time
where the time goes in v4:
time: 101 us; the launch traced here: 99.7 us
  Pallas kernels  99.1 us (98%)
    pallas_call x1, Pallas kernels, per_device(): pl.pallas_call(kernel, out_shape=shapes, in_specs=[hbm] * 9, out_specs=(v...  97.2 us

profile of v4, /device:TPU:22, one launch (start us, length us, event | category | flops | bytes accessed | tf_op | source)
XLA Modules:
  0.0 99.7 jit_solution(14055553649118179351)
XLA Ops:
  0.6 97.2 %shard_map.144 = (bf16[512,256]{1,0:T(8,128)(2,1)}, bf16[512,256]{1,0:T(8,128)(2,1)}, f32[2,8]{1,0:T(2,128)}, f32[8,768]{1,0:T(8,128)}, f32[8,256]{1,0:T(8,128)}, /*index=5*/f32[8,1024]{1,0:T(8,128)}, f32[32,256]{1,0:T(8,128)}) custom-call(s32[1,512]{1,0:T(1,128)} %bitcast.2, s32[1,512]{1,0:T(1,128)} %bitcast.3, bf16[512,256]{1,0:T(8,128)(2,1)} %features_ref.1, ...), custom_call_target="tpu_custom_call" | custom-call | tf_op jit(solution)/shard_map/pallas_call | solution.py:468
  97.8 1.9 %shard_map.145 = (bf16[512,256]{1,0:T(8,128)(2,1)}, bf16[512,256]{1,0:T(8,128)(2,1)}, f32[2,8]{1,0:T(2,128)}, f32[8,768]{1,0:T(8,128)}, f32[8,256]{1,0:T(8,128)}, /*index=5*/f32[8,1024]{1,0:T(8,128)}, f32[32,256]{1,0:T(8,128)}) custom-call(bf16[512,256]{1,0:T(8,128)(2,1)} %get-tuple-element.14.refs_0_, bf16[512,256]{1,0:T(8,128)(2,1)} %get-tuple-element.15.refs_1_, ...), custom_call_target="tpu_custom_call" | custom-call | tf_op jit(solution)/shard_map/pallas_call | solution.py:478

commit v5 on v4

--- a/solution.py
+++ b/solution.py
@@ -149,7 +149,7 @@
         s.dqkv[pl.ds(rows + D, HD), :] = (nt(query, ds) * SCALE).astype(bf16)
         s.dqkv[pl.ds(rows, HD), :] = (nn(key, ds) * SCALE).astype(bf16)
 
-    heads_loop(head)
+    heads_loop(head, HEADS)
     dn1 = nn(s.qkv_w[b], s.dqkv[...]).astype(bf16).astype(f32)
     s.dn1[...] = dn1
     return (s.da[...] + norm_back(dn1, s.xh1[b], s.r1[b], s.gain[2 * b][:, 0:1])).astype(bf16)

time: 101 us -> 100 us (0.990); the launches traced: 99.7 us -> 99.8 us
  no operation moved by 1% of the time
where the time goes in v5:
time: 100 us; the launch traced here: 99.8 us
  Pallas kernels  99.2 us (99%)
    pallas_call x1, Pallas kernels, per_device(): pl.pallas_call(kernel, out_shape=shapes, in_specs=[hbm] * 9, out_specs=(v...  97.3 us

profile of v5, /device:TPU:22, one launch (start us, length us, event | category | flops | bytes accessed | tf_op | source)
XLA Modules:
  0.0 99.8 jit_solution(8007891832438698680)
XLA Ops:
  0.6 97.3 %shard_map.144 = (bf16[512,256]{1,0:T(8,128)(2,1)}, bf16[512,256]{1,0:T(8,128)(2,1)}, f32[2,8]{1,0:T(2,128)}, f32[8,768]{1,0:T(8,128)}, f32[8,256]{1,0:T(8,128)}, /*index=5*/f32[8,1024]{1,0:T(8,128)}, f32[32,256]{1,0:T(8,128)}) custom-call(s32[1,512]{1,0:T(1,128)} %bitcast.2, s32[1,512]{1,0:T(1,128)} %bitcast.3, bf16[512,256]{1,0:T(8,128)(2,1)} %features_ref.1, ...), custom_call_target="tpu_custom_call" | custom-call | tf_op jit(solution)/shard_map/pallas_call | solution.py:468
  97.9 1.9 %shard_map.145 = (bf16[512,256]{1,0:T(8,128)(2,1)}, bf16[512,256]{1,0:T(8,128)(2,1)}, f32[2,8]{1,0:T(2,128)}, f32[8,768]{1,0:T(8,128)}, f32[8,256]{1,0:T(8,128)}, /*index=5*/f32[8,1024]{1,0:T(8,128)}, f32[32,256]{1,0:T(8,128)}) custom-call(bf16[512,256]{1,0:T(8,128)(2,1)} %get-tuple-element.14.refs_0_, bf16[512,256]{1,0:T(8,128)(2,1)} %get-tuple-element.15.refs_1_, ...), custom_call_target="tpu_custom_call" | custom-call | tf_op jit(solution)/shard_map/pallas_call | solution.py:478
